TPU v7x, 32 devices: a whole 2x2x4 slice. The times are simulated.
32 devices in a mesh: pool: 2 (over y), rep: 4 (over z), tp: 4 (over x, core).
Axes of the slice: x: 2, y: 2, z: 4, core: 2. Of those that a mesh axis runs over, the one named last changes fastest.
Arguments:
- hidden: bfloat16 [64, 8192], P(('pool', 'rep'), 'tp'), parts along dimension 0, may hold values from -6 to 6
- base_query_proj: bfloat16 [64, 8192], P(('pool', 'rep'), 'tp'), parts along dimension 0, may hold values from -10 to 10
- base_key_proj: bfloat16 [64, 1024], P(('pool', 'rep'), 'tp'), parts along dimension 0, may hold values from -6 to 6
- base_value_proj: bfloat16 [64, 1024], P(('pool', 'rep'), 'tp'), parts along dimension 0, may hold values from -6 to 6
- key_cache: bfloat16 [64, 512, 1024], P(('pool', 'rep'), None, 'tp'), parts along dimension 0, may hold values from -10 to 10
- value_cache: bfloat16 [64, 512, 1024], P(('pool', 'rep'), None, 'tp'), parts along dimension 0, may hold values from -6 to 6
- lengths: int32 [64], P('pool'), parts along dimension 0, may hold values from 2 to 511, as said below
- adapter_down_factors: bfloat16 [16, 8192, 192], P(('pool', 'rep'), 'tp'), parts along dimension 0, may hold values from -0.0625 to 0.0625
- adapter_up_query: bfloat16 [16, 64, 8192], P(('pool', 'rep'), None, 'tp'), parts along dimension 0, may hold values from -0.75 to 0.75
- adapter_up_key_value: bfloat16 [16, 2, 64, 1024], P(('pool', 'rep'), None, None, 'tp'), parts along dimension 0, may hold values from -0.75 to 0.75
- resident: int32 [8, 2], P('pool'), parts along dimension 0, may hold values from 0 to 63, as said below
- request_adapter_id: int32 [64], P(('pool', 'rep')), parts along dimension 0, may hold values from 0 to 63, as said below
- migration_offset: int32 [4], P('pool'), parts along dimension 0, may hold values from 1 to 3, as said below
Outputs:
- attended: bfloat16 [64, 8192], P(('pool', 'rep'), 'tp'), parts along dimension 0
- moved_keys: bfloat16 [16, 512, 1024], P(('pool', 'rep'), None, 'tp'), parts along dimension 0
- moved_values: bfloat16 [16, 512, 1024], P(('pool', 'rep'), None, 'tp'), parts along dimension 0
- arrived_down_factors: bfloat16 [16, 8192, 192], P(('pool', 'rep'), 'tp'), parts along dimension 0
- arrived_up_query: bfloat16 [16, 64, 8192], P(('pool', 'rep'), None, 'tp'), parts along dimension 0
- arrived_up_key_value: bfloat16 [16, 2, 64, 1024], P(('pool', 'rep'), None, None, 'tp'), parts along dimension 0
There are 2 independent parts, one for each index of `pool`. A program takes and returns all parts, laid end to end along the dimension named above; each array names one. Nothing has to cross between parts.
Inputs may be any that keep to these rules, and one draw needn't show every extreme that they name: `lengths`: one request in every draw has exactly 511 cached positions. `resident`: the ids loaded on one replica all differ. `request_adapter_id`: every request's adapter is loaded on the replica that holds it on entry. `migration_offset`: all offsets differ.
All inputs are finite; a program needn't handle non-finite values.
Results may differ from a plain program's by a relative error of at most 0.0076.
Values may be sent and summed in bfloat16 or wider, within the bound.
No kernel may reach another device: no remote copies, remote signals or barrier semaphores. Data moves between devices by JAX's collectives and lax.ppermute only.
A program may use at most 64 MiB of HBM per device.

v0:
```python
import math

import jax
import jax.numpy as jnp
from jax import lax
from jax.sharding import PartitionSpec as P

HEAD_SIZE = 128


def shifted(shard, axis, by):
    size = lax.axis_size(axis)
    return lax.ppermute(shard, axis, [(i, (i + by) % size) for i in range(size)])


def attend(query, keys, value_rows, key_new, value_new, lengths_now):
    batch_rows = query.shape[0]
    positions = keys.shape[1]
    kv_heads = key_new.shape[1] // HEAD_SIZE
    group_size = query.shape[1] // (kv_heads * HEAD_SIZE)
    factor = 1.0 / math.sqrt(HEAD_SIZE)
    q_heads = query.reshape(batch_rows, kv_heads, group_size, HEAD_SIZE)
    k_heads = keys.reshape(batch_rows, positions, kv_heads, HEAD_SIZE)
    v_heads = value_rows.reshape(batch_rows, positions, kv_heads, HEAD_SIZE)
    new_keys = key_new.reshape(batch_rows, kv_heads, HEAD_SIZE)
    new_values = value_new.reshape(batch_rows, kv_heads, HEAD_SIZE).astype(jnp.float32)
    scores = (
        jnp.einsum("nhgd,nthd->nhgt", q_heads, k_heads, preferred_element_type=jnp.float32) * factor
    )
    fresh = (
        jnp.einsum("nhgd,nhd->nhg", q_heads, new_keys, preferred_element_type=jnp.float32) * factor
    )
    valid = (jnp.arange(positions, dtype=jnp.int32)[None, :] < lengths_now[:, None])[
        :, None, None, :
    ]
    peak = jnp.maximum(jnp.max(jnp.where(valid, scores, -1e30), axis=-1), fresh)
    raised = jnp.where(valid, jnp.exp(scores - peak[..., None]), 0.0)
    raised_new = jnp.exp(fresh - peak)
    total = jnp.sum(raised, axis=-1) + raised_new
    weights = (raised / total[..., None]).astype(jnp.bfloat16)
    weight_new = (raised_new / total).astype(jnp.bfloat16)
    mixed = jnp.einsum("nhgt,nthd->nhgd", weights, v_heads, preferred_element_type=jnp.float32)
    mixed = mixed + weight_new.astype(jnp.float32)[..., None] * new_values[:, :, None, :]
    return mixed.reshape(batch_rows, -1).astype(jnp.bfloat16)


def pick_sum(indicator_matrix, every):
    return jnp.sum(indicator_matrix[:, :, None] * every, axis=1)


def rank_total(partial_rows):
    return lax.psum(partial_rows, "tp").astype(jnp.bfloat16)


def adapter_row_ids(shrunk_part, base_rows, up_factor, indicator_matrix):
    every = jnp.einsum("rk,akc->rac", shrunk_part, up_factor, preferred_element_type=jnp.float32)
    return (base_rows.astype(jnp.float32) + pick_sum(indicator_matrix, every)).astype(jnp.bfloat16)


def adapt_all(
    hidden,
    base_query_proj,
    base_key_proj,
    base_value_proj,
    adapter_down_factors,
    adapter_up_query,
    adapter_up_key_value,
    indicator_matrix,
    rank_extent,
):
    every = jnp.einsum(
        "wb,xbm->wxm", hidden, adapter_down_factors, preferred_element_type=jnp.float32
    )
    shrunk = rank_total(pick_sum(indicator_matrix, every))
    query = adapter_row_ids(
        shrunk[:, :rank_extent], base_query_proj, adapter_up_query, indicator_matrix
    )
    key_new = adapter_row_ids(
        shrunk[:, rank_extent : 2 * rank_extent],
        base_key_proj,
        adapter_up_key_value[:, 0],
        indicator_matrix,
    )
    value_new = adapter_row_ids(
        shrunk[:, 2 * rank_extent :], base_value_proj, adapter_up_key_value[:, 1], indicator_matrix
    )
    return (query, key_new, value_new)


def factor_row_list(select_rows, adapter_down_factors, adapter_up_query, adapter_up_key_value):
    down_rows = jnp.einsum(
        "zi,iqf->zqf", select_rows, adapter_down_factors, preferred_element_type=jnp.float32
    ).astype(jnp.bfloat16)
    upq_rows = jnp.einsum(
        "zj,juq->zuq", select_rows, adapter_up_query, preferred_element_type=jnp.float32
    ).astype(jnp.bfloat16)
    upkv_rows = jnp.einsum(
        "nx,xvuy->nvuy", select_rows, adapter_up_key_value, preferred_element_type=jnp.float32
    ).astype(jnp.bfloat16)
    return (down_rows, upq_rows, upkv_rows)


def write_entry(cache_rows, entry_rows, spots):
    place = (jnp.arange(cache_rows.shape[1], dtype=jnp.int32)[None, :] == spots[:, None])[
        :, :, None
    ]
    return jnp.where(place, entry_rows[:, None, :], cache_rows)


def settle(payload, moved, migration_offset, bit_level):
    move_flags = jnp.right_shift(migration_offset, bit_level) % 2 == 1
    return tuple(
        (
            jnp.where(move_flags.reshape((-1,) + (1,) * (stay_part.ndim - 1)), came_part, stay_part)
            for stay_part, came_part in zip(payload, moved)
        )
    )


def local(
    hidden,
    base_query_proj,
    base_key_proj,
    base_value_proj,
    key_cache,
    value_cache,
    lengths,
    adapter_down_factors,
    adapter_up_query,
    adapter_up_key_value,
    resident,
    request_adapter_id,
    migration_offset,
):
    count_of_rows = hidden.shape[0]
    moving = migration_offset.shape[0]
    remaining_requests = count_of_rows - moving
    rank_extent = adapter_up_query.shape[1]
    devices = lax.axis_size("rep")
    my_index = lax.axis_index("rep")
    hop_count = devices.bit_length() - 1
    res_row = lax.dynamic_index_in_dim(resident, my_index, 0, keepdims=False)
    indicator_matrix = (request_adapter_id[:, None] == res_row[None, :]).astype(jnp.float32)
    all_lengths = lax.dynamic_slice_in_dim(lengths, my_index * count_of_rows, count_of_rows)
    down_rows, upq_rows, upkv_rows = factor_row_list(
        indicator_matrix[remaining_requests:].astype(jnp.bfloat16),
        adapter_down_factors,
        adapter_up_query,
        adapter_up_key_value,
    )
    query, key_new, value_new = adapt_all(
        hidden,
        base_query_proj,
        base_key_proj,
        base_value_proj,
        adapter_down_factors,
        adapter_up_query,
        adapter_up_key_value,
        indicator_matrix,
        rank_extent,
    )
    completed = attend(query, key_cache, value_cache, key_new, value_new, all_lengths)
    written_keys = write_entry(
        key_cache[remaining_requests:],
        key_new[remaining_requests:],
        all_lengths[remaining_requests:],
    )
    written_values = write_entry(
        value_cache[remaining_requests:],
        value_new[remaining_requests:],
        all_lengths[remaining_requests:],
    )
    payload = (
        completed[remaining_requests:],
        written_keys,
        written_values,
        down_rows,
        upq_rows,
        upkv_rows,
    )
    for bit_level in range(hop_count):
        moved = shifted(
            (payload[0], payload[1], payload[2], payload[3], payload[4], payload[5]),
            "rep",
            1 << bit_level,
        )
        payload = settle(payload, moved, migration_offset, bit_level)
    (
        carried_out,
        moved_keys,
        moved_values,
        arrived_down_factors,
        arrived_up_query,
        arrived_up_key_value,
    ) = payload
    attended = jnp.concatenate([completed[:remaining_requests], carried_out], axis=0)
    return (
        attended,
        moved_keys,
        moved_values,
        arrived_down_factors,
        arrived_up_query,
        arrived_up_key_value,
    )


def solution(mesh):
    placed = (
        P(("pool", "rep"), "tp"),
        P(("pool", "rep"), "tp"),
        P(("pool", "rep"), "tp"),
        P(("pool", "rep"), "tp"),
        P(("pool", "rep"), None, "tp"),
        P(("pool", "rep"), None, "tp"),
        P("pool"),
        P(("pool", "rep"), "tp", None),
        P(("pool", "rep"), None, "tp"),
        P(("pool", "rep"), None, None, "tp"),
        P("pool", None),
        P(("pool", "rep")),
        P("pool"),
    )
    return jax.shard_map(
        local,
        mesh=mesh,
        in_specs=placed,
        out_specs=(
            P(("pool", "rep"), "tp"),
            P(("pool", "rep"), None, "tp"),
            P(("pool", "rep"), None, "tp"),
            P(("pool", "rep"), "tp", None),
            P(("pool", "rep"), None, "tp"),
            P(("pool", "rep"), None, None, "tp"),
        ),
        check_vma=False,
    )
```

profile of v0, /device:TPU:0, one launch (start us, length us, event | category | flops | bytes accessed | tf_op | source)
XLA Modules:
  0.0 237.0 jit_solution(5320845059608062864)
XLA Ops:
  0.7 1.0 dynamic-slice_reduce_fusion
  1.7 0.7 fusion.37
  2.4 0.1 copy.19
  2.5 1.3 fusion.17
  3.8 8.6 %psum.7 = bf16[8,192]{1,0:T(8,128)(2,1)S(1)} all-reduce(f32[8,192]{1,0:T(8,128)S(1)} %fusion.17), channel_id=1, replica_groups=mesh['pool'=2,'rep'=4,'tp'=4] {'tp'}, use_global_device_ids=true, to_apply=%region_1.2 | all-reduce | flops 1536 | bytes 9216 | tf_op jit(solution)/shard_map/psum | solution.py:52
  12.4 0.1 fusion.19
  12.5 0.2 fusion.18
  13.0 1.5 slice_select_fusion
  14.6 1.6 collective-permute-start.2
  16.2 1.6 collective-permute-start.4
  17.9 0.2 fusion.10
  18.1 0.1 fusion.32
  18.2 0.7 select_reduce_fusion
  19.0 0.2 fusion.21
  19.2 0.4 copy-done.3
  19.6 0.4 fusion.14
  20.1 1.6 collective-permute-start
  21.7 1.8 convolution_convert_fusion
  23.5 0.3 collective-permute-start.6
  23.8 0.7 convolution_convert_fusion.1
  24.5 1.6 collective-permute-start.8
  26.1 0.3 convolution_convert_fusion.2
  26.5 16.3 %collective-permute-done = bf16[2,2048]{1,0:T(2,128)(2,1)S(1)} collective-permute-done((bf16[2,2048]{1,0:T(2,128)(2,1)S(1)}, bf16[2,2048]{1,0:T(2,128)(2,1)S(1)}, u32[]{:S(2)}, u32[]{:S(2)}) %collective-permute-start) | collective-permute-done | bytes 8224 | tf_op jit(solution)/shard_map/ppermute | solution.py:13
  42.8 0.1 broadcast_select_fusion.10
  42.9 0.8 collective-permute-start.1
  43.6 43.3 %collective-permute-done.1 = bf16[2,2048]{1,0:T(2,128)(2,1)S(1)} collective-permute-done((bf16[2,2048]{1,0:T(2,128)(2,1)S(1)}, bf16[2,2048]{1,0:T(2,128)(2,1)S(1)}, u32[]{:S(2)}, u32[]{:S(2)}) %collective-permute-start.1) | collective-permute-done | bytes 8224 | tf_op jit(solution)/shard_map/ppermute | solution.py:13
  87.0 0.1 broadcast_select_fusion.11
  87.1 0.6 pad_maximum_fusion
  87.7 6.1 %collective-permute-done.10 = bf16[2,2,64,256]{3,0,2,1:T(2,128)(2,1)S(1)} collective-permute-done((bf16[2,2,64,256]{3,0,2,1:T(2,128)(2,1)S(1)}, bf16[2,2,64,256]{3,0,2,1:T(2,128)(2,1)S(1)}, u32[]{:S(2)}, u32[]{:S(2)}) %collective-permute-start.10) | collective-permute-done | bytes 131104 | tf_op jit(solution)/shard_map/ppermute | solution.py:13
  93.8 0.2 broadcast_select_fusion.8
  94.1 1.7 broadcast_select_fusion
  95.8 3.0 %collective-permute-start.7 = (bf16[2,2048,192]{1,0,2:T(2,128)(2,1)S(1)}, bf16[2,2048,192]{1,0,2:T(2,128)(2,1)S(1)}, u32[]{:S(2)}, u32[]{:S(2)}) collective-permute-start(bf16[2,2048,192]{1,0,2:T(2,128)(2,1)S(1)} %broadcast_select_fusion), channel_id=1, source_target_pairs={{0,8},{4,12},{8,0},{12,4},{1,9},{5,13},{9,1},{13,5},{2,10},{6,14},... | collective-permute-start | bytes 4718600 | tf_op jit(solution)/shard_map/ppermute | solution.py:13
  98.8 0.6 broadcast_select_fusion.2
  99.4 0.1 collective-permute-start.9
  99.5 0.2 broadcast_select_fusion.4
  99.7 3.0 %collective-permute-start.3 = (bf16[2,512,256]{2,1,0:T(8,128)(2,1)S(1)}, bf16[2,512,256]{2,1,0:T(8,128)(2,1)S(1)}, u32[]{:S(2)}, u32[]{:S(2)}) collective-permute-start(bf16[2,512,256]{2,1,0:T(8,128)(2,1)S(1)} %get-tuple-element.23), channel_id=1, source_target_pairs={{0,8},{4,12},{8,0},{12,4},{1,9},{5,13},{9,1},{13,5},{2,10},{6,14},... | collective-permute-start | bytes 1572872 | tf_op jit(solution)/shard_map/ppermute | solution.py:13
  102.7 0.1 collective-permute-start.5
  102.7 62.7 %collective-permute-done.11 = bf16[2,2,64,256]{3,0,2,1:T(2,128)(2,1)S(1)} collective-permute-done((bf16[2,2,64,256]{3,0,2,1:T(2,128)(2,1)S(1)}, bf16[2,2,64,256]{3,0,2,1:T(2,128)(2,1)S(1)}, u32[]{:S(2)}, u32[]{:S(2)}) %collective-permute-start.11) | collective-permute-done | bytes 131104 | tf_op jit(solution)/shard_map/ppermute | solution.py:13
  165.4 0.2 broadcast_select_fusion.9
  165.7 0.7 copy.33
  166.3 44.0 %collective-permute-done.9 = bf16[2,64,2048]{2,0,1:T(2,128)(2,1)S(1)} collective-permute-done((bf16[2,64,2048]{2,0,1:T(2,128)(2,1)S(1)}, bf16[2,64,2048]{2,0,1:T(2,128)(2,1)S(1)}, u32[]{:S(2)}, u32[]{:S(2)}) %collective-permute-start.9) | collective-permute-done | bytes 524320 | tf_op jit(solution)/shard_map/ppermute | solution.py:13
  210.4 0.6 broadcast_select_fusion.3
  211.0 1.0 copy.32
  212.0 9.6 %collective-permute-done.3 = bf16[2,512,256]{2,1,0:T(8,128)(2,1)S(1)} collective-permute-done((bf16[2,512,256]{2,1,0:T(8,128)(2,1)S(1)}, bf16[2,512,256]{2,1,0:T(8,128)(2,1)S(1)}, u32[]{:S(2)}, u32[]{:S(2)}) %collective-permute-start.3) | collective-permute-done | bytes 524320 | tf_op jit(solution)/shard_map/ppermute | solution.py:13
  221.6 10.7 %collective-permute-done.5 = bf16[2,512,256]{2,1,0:T(8,128)(2,1)S(1)} collective-permute-done((bf16[2,512,256]{2,1,0:T(8,128)(2,1)S(1)}, bf16[2,512,256]{2,1,0:T(8,128)(2,1)S(1)}, u32[]{:S(2)}, u32[]{:S(2)}) %collective-permute-start.5) | collective-permute-done | bytes 524320 | tf_op jit(solution)/shard_map/ppermute | solution.py:13
  232.4 1.1 broadcast_select_fusion.6
  233.5 1.7 broadcast_select_fusion.1
  235.2 1.8 copy.31
  (43 shorter events, 0.6 us)
Async XLA Ops:
  0.6 1.9 copy-start
  0.6 11.8 %copy-start.7 = (bf16[2,2,64,256]{3,2,1,0:T(8,128)(2,1)S(1)}, bf16[2,2,64,256]{3,2,1,0:T(8,128)(2,1)}, u32[]{:S(2)}) copy-start(bf16[2,2,64,256]{3,2,1,0:T(8,128)(2,1)} %param.22) | copy-start | bytes 393220
  0.7 12.1 %copy-start.5 = (bf16[8,256]{1,0:T(8,128)(2,1)S(1)}, bf16[8,256]{1,0:T(8,128)(2,1)}, u32[]{:S(2)}) copy-start(bf16[8,256]{1,0:T(8,128)(2,1)} %param.16) | copy-start | bytes 12292
  0.7 12.1 %copy-start.6 = (bf16[8,256]{1,0:T(8,128)(2,1)S(1)}, bf16[8,256]{1,0:T(8,128)(2,1)}, u32[]{:S(2)}) copy-start(bf16[8,256]{1,0:T(8,128)(2,1)} %param.15) | copy-start | bytes 12292
  0.7 12.1 %copy-start.8 = (s32[32]{0:T(128)S(1)}, s32[32]{0:T(128)}, u32[]{:S(2)}) copy-start(s32[32]{0:T(128)} %param.19) | copy-start | bytes 388
  3.8 14.1 %copy-start.2 = (bf16[2,64,2048]{2,1,0:T(8,128)(2,1)S(1)}, bf16[2,64,2048]{2,1,0:T(8,128)(2,1)}, u32[]{:S(2)}) copy-start(bf16[2,64,2048]{2,1,0:T(8,128)(2,1)} %param.21) | copy-start | bytes 1572868
  3.8 14.3 %copy-start.4 = (bf16[8,2048]{1,0:T(8,128)(2,1)S(1)}, bf16[8,2048]{1,0:T(8,128)(2,1)}, u32[]{:S(2)}) copy-start(bf16[8,2048]{1,0:T(8,128)(2,1)} %param.14) | copy-start | bytes 98308
  12.8 5.4 %copy-start.1 = (bf16[8,512,256]{2,1,0:T(8,128)(2,1)S(1)}, bf16[8,512,256]{2,1,0:T(8,128)(2,1)}, u32[]{:S(2)}) copy-start(bf16[8,512,256]{2,1,0:T(8,128)(2,1)} %param.17) | copy-start | bytes 6291460
  14.6 85.0 %collective-permute-start.2 = (bf16[2,512,256]{2,1,0:T(8,128)(2,1)S(1)}, bf16[2,512,256]{2,1,0:T(8,128)(2,1)S(1)}, u32[]{:S(2)}, u32[]{:S(2)}) collective-permute-start(bf16[2,512,256]{2,1,0:T(8,128)(2,1)S(1)} %get-tuple-element.17), channel_id=1, source_target_pairs={{0,4},{4,8},{8,12},{12,0},{1,5},{5,9},{9,13},{13,1},{2,6},{6,10},{... | collective-permute-start | bytes 1572872 | tf_op jit(solution)/shard_map/ppermute | solution.py:13
  16.2 83.3 %collective-permute-start.4 = (bf16[2,512,256]{2,1,0:T(8,128)(2,1)S(1)}, bf16[2,512,256]{2,1,0:T(8,128)(2,1)S(1)}, u32[]{:S(2)}, u32[]{:S(2)}) collective-permute-start(bf16[2,512,256]{2,1,0:T(8,128)(2,1)S(1)} %get-tuple-element.16), channel_id=1, source_target_pairs={{0,4},{4,8},{8,12},{12,0},{1,5},{5,9},{9,13},{13,1},{2,6},{6,10},{... | collective-permute-start | bytes 1572872 | tf_op jit(solution)/shard_map/ppermute | solution.py:13
  18.1 1.6 copy-start.3
  20.1 22.7 %collective-permute-start = (bf16[2,2048]{1,0:T(2,128)(2,1)S(1)}, bf16[2,2048]{1,0:T(2,128)(2,1)S(1)}, u32[]{:S(2)}, u32[]{:S(2)}) collective-permute-start(bf16[2,2048]{1,0:T(2,128)(2,1)S(1)} %bitcast.84), channel_id=1, source_target_pairs={{0,4},{4,8},{8,12},{12,0},{1,5},{5,9},{9,13},{13,1},{2,6},{6,10},{... | collective-permute-start | bytes 24584 | tf_op jit(solution)/shard_map/ppermute | solution.py:13
  23.5 2.9 %copy-start.9 = (s32[2]{0:T(128)S(1)}, s32[2]{0:T(128)}, u32[]{:S(2)}) copy-start(s32[2]{0:T(128)} %param.25) | copy-start | bytes 28
  23.5 70.6 %collective-permute-start.6 = (bf16[2,2048,192]{1,0,2:T(2,128)(2,1)S(1)}, bf16[2,2048,192]{1,0,2:T(2,128)(2,1)S(1)}, u32[]{:S(2)}, u32[]{:S(2)}) collective-permute-start(bf16[2,2048,192]{1,0,2:T(2,128)(2,1)S(1)} %convolution_convert_fusion), channel_id=1, source_target_pairs={{0,4},{4,8},{8,12},{12,0},{1,5},{5,9},{9,13},{13,1},{2,6},{6,10},{... | collective-permute-start | bytes 4718600 | tf_op jit(solution)/shard_map/ppermute | solution.py:13
  24.5 74.3 %collective-permute-start.8 = (bf16[2,64,2048]{2,0,1:T(2,128)(2,1)S(1)}, bf16[2,64,2048]{2,0,1:T(2,128)(2,1)S(1)}, u32[]{:S(2)}, u32[]{:S(2)}) collective-permute-start(bf16[2,64,2048]{2,0,1:T(2,128)(2,1)S(1)} %convolution_convert_fusion.1), channel_id=1, source_target_pairs={{0,4},{4,8},{8,12},{12,0},{1,5},{5,9},{9,13},{13,1},{2,6},{6,10},{... | collective-permute-start | bytes 1572872 | tf_op jit(solution)/shard_map/ppermute | solution.py:13
  42.9 44.1 %collective-permute-start.1 = (bf16[2,2048]{1,0:T(2,128)(2,1)S(1)}, bf16[2,2048]{1,0:T(2,128)(2,1)S(1)}, u32[]{:S(2)}, u32[]{:S(2)}) collective-permute-start(bf16[2,2048]{1,0:T(2,128)(2,1)S(1)} %broadcast_select_fusion.10), channel_id=1, source_target_pairs={{0,8},{4,12},{8,0},{12,4},{1,9},{5,13},{9,1},{13,5},{2,10},{6,14},... | collective-permute-start | bytes 24584 | tf_op jit(solution)/shard_map/ppermute | solution.py:13
  87.0 6.8 %collective-permute-start.10 = (bf16[2,2,64,256]{3,0,2,1:T(2,128)(2,1)S(1)}, bf16[2,2,64,256]{3,0,2,1:T(2,128)(2,1)S(1)}, u32[]{:S(2)}, u32[]{:S(2)}) collective-permute-start(bf16[2,2,64,256]{3,0,2,1:T(2,128)(2,1)S(1)} %convolution_convert_fusion.2), channel_id=1, source_target_pairs={{0,4},{4,8},{8,12},{12,0},{1,5},{5,9},{9,13},{13,1},{2,6},{6,10},{... | collective-permute-start | bytes 393224 | tf_op jit(solution)/shard_map/ppermute | solution.py:13
  94.0 71.4 %collective-permute-start.11 = (bf16[2,2,64,256]{3,0,2,1:T(2,128)(2,1)S(1)}, bf16[2,2,64,256]{3,0,2,1:T(2,128)(2,1)S(1)}, u32[]{:S(2)}, u32[]{:S(2)}) collective-permute-start(bf16[2,2,64,256]{3,0,2,1:T(2,128)(2,1)S(1)} %broadcast_select_fusion.8), channel_id=1, source_target_pairs={{0,8},{4,12},{8,0},{12,4},{1,9},{5,13},{9,1},{13,5},{2,10},{6,14},... | collective-permute-start | bytes 393224 | tf_op jit(solution)/shard_map/ppermute | solution.py:13
  95.8 137.7 %collective-permute-start.7 = (bf16[2,2048,192]{1,0,2:T(2,128)(2,1)S(1)}, bf16[2,2048,192]{1,0,2:T(2,128)(2,1)S(1)}, u32[]{:S(2)}, u32[]{:S(2)}) collective-permute-start(bf16[2,2048,192]{1,0,2:T(2,128)(2,1)S(1)} %broadcast_select_fusion), channel_id=1, source_target_pairs={{0,8},{4,12},{8,0},{12,4},{1,9},{5,13},{9,1},{13,5},{2,10},{6,14},... | collective-permute-start | bytes 4718600 | tf_op jit(solution)/shard_map/ppermute | solution.py:13
  99.4 111.0 %collective-permute-start.9 = (bf16[2,64,2048]{2,0,1:T(2,128)(2,1)S(1)}, bf16[2,64,2048]{2,0,1:T(2,128)(2,1)S(1)}, u32[]{:S(2)}, u32[]{:S(2)}) collective-permute-start(bf16[2,64,2048]{2,0,1:T(2,128)(2,1)S(1)} %broadcast_select_fusion.2), channel_id=1, source_target_pairs={{0,8},{4,12},{8,0},{12,4},{1,9},{5,13},{9,1},{13,5},{2,10},{6,14},... | collective-permute-start | bytes 1572872 | tf_op jit(solution)/shard_map/ppermute | solution.py:13
  99.7 121.9 %collective-permute-start.3 = (bf16[2,512,256]{2,1,0:T(8,128)(2,1)S(1)}, bf16[2,512,256]{2,1,0:T(8,128)(2,1)S(1)}, u32[]{:S(2)}, u32[]{:S(2)}) collective-permute-start(bf16[2,512,256]{2,1,0:T(8,128)(2,1)S(1)} %get-tuple-element.23), channel_id=1, source_target_pairs={{0,8},{4,12},{8,0},{12,4},{1,9},{5,13},{9,1},{13,5},{2,10},{6,14},... | collective-permute-start | bytes 1572872 | tf_op jit(solution)/shard_map/ppermute | solution.py:13
  102.7 129.7 %collective-permute-start.5 = (bf16[2,512,256]{2,1,0:T(8,128)(2,1)S(1)}, bf16[2,512,256]{2,1,0:T(8,128)(2,1)S(1)}, u32[]{:S(2)}, u32[]{:S(2)}) collective-permute-start(bf16[2,512,256]{2,1,0:T(8,128)(2,1)S(1)} %get-tuple-element.22), channel_id=1, source_target_pairs={{0,8},{4,12},{8,0},{12,4},{1,9},{5,13},{9,1},{13,5},{2,10},{6,14},... | collective-permute-start | bytes 1572872 | tf_op jit(solution)/shard_map/ppermute | solution.py:13
where the time goes:
time: 237 us
  waiting for transfers between devices  193 us (81%)
  starting transfers between devices  13.7 us (6%)
  other arithmetic  9.9 us (4%)
  blocking collectives  8.62 us (4%)
  matrix products  5.8 us (2%)
  local copies, waits for them, and re-layouts  5.13 us (2%)
    ppermute x12, waiting for transfers between devices, shifted(): lax.ppermute(shard, axis, [(i, (i + by) % size) for i in range(size)])  193 us
    ppermute x12, starting transfers between devices, shifted(): lax.ppermute(shard, axis, [(i, (i + by) % size) for i in range(size)])  13.7 us
    psum x1, blocking collectives, rank_total(): return lax.psum(partial_rows, 'tp').astype(jnp.bfloat16)  8.62 us
    select_n x10, other arithmetic, settle(): jnp.where(move_flags.reshape((-1,) + (1,) * (stay_part.ndim - 1)), came_p...  6.59 us
  transfers between devices with their start and end apart: 12, of which 7 were waited for; matrix products, arithmetic and copies ran while one was open for 5% of the time, Pallas kernels for 0%

commit v1 on v0

--- a/solution.py
+++ b/solution.py
@@ -1,3 +1,4 @@
+import itertools
 import math
 
 import jax
@@ -6,6 +7,7 @@
 from jax.sharding import PartitionSpec as P
 
 HEAD_SIZE = 128
+MOST_JOINT_BRANCHES = 6
 
 
 def shifted(shard, axis, by):
@@ -87,34 +89,8 @@
     return (query, key_new, value_new)
 
 
-def factor_row_list(select_rows, adapter_down_factors, adapter_up_query, adapter_up_key_value):
-    down_rows = jnp.einsum(
-        "zi,iqf->zqf", select_rows, adapter_down_factors, preferred_element_type=jnp.float32
-    ).astype(jnp.bfloat16)
-    upq_rows = jnp.einsum(
-        "zj,juq->zuq", select_rows, adapter_up_query, preferred_element_type=jnp.float32
-    ).astype(jnp.bfloat16)
-    upkv_rows = jnp.einsum(
-        "nx,xvuy->nvuy", select_rows, adapter_up_key_value, preferred_element_type=jnp.float32
-    ).astype(jnp.bfloat16)
-    return (down_rows, upq_rows, upkv_rows)
-
-
-def write_entry(cache_rows, entry_rows, spots):
-    place = (jnp.arange(cache_rows.shape[1], dtype=jnp.int32)[None, :] == spots[:, None])[
-        :, :, None
-    ]
-    return jnp.where(place, entry_rows[:, None, :], cache_rows)
-
-
-def settle(payload, moved, migration_offset, bit_level):
-    move_flags = jnp.right_shift(migration_offset, bit_level) % 2 == 1
-    return tuple(
-        (
-            jnp.where(move_flags.reshape((-1,) + (1,) * (stay_part.ndim - 1)), came_part, stay_part)
-            for stay_part, came_part in zip(payload, moved)
-        )
-    )
+def pick(array, at):
+    return lax.dynamic_index_in_dim(array, at, 0, keepdims=False)
 
 
 def local(
@@ -132,76 +108,127 @@
     request_adapter_id,
     migration_offset,
 ):
-    count_of_rows = hidden.shape[0]
+    count = hidden.shape[0]
     moving = migration_offset.shape[0]
-    remaining_requests = count_of_rows - moving
+    stay = count - moving
     rank_extent = adapter_up_query.shape[1]
-    devices = lax.axis_size("rep")
-    my_index = lax.axis_index("rep")
-    hop_count = devices.bit_length() - 1
-    res_row = lax.dynamic_index_in_dim(resident, my_index, 0, keepdims=False)
-    indicator_matrix = (request_adapter_id[:, None] == res_row[None, :]).astype(jnp.float32)
-    all_lengths = lax.dynamic_slice_in_dim(lengths, my_index * count_of_rows, count_of_rows)
-    down_rows, upq_rows, upkv_rows = factor_row_list(
-        indicator_matrix[remaining_requests:].astype(jnp.bfloat16),
-        adapter_down_factors,
-        adapter_up_query,
-        adapter_up_key_value,
-    )
-    query, key_new, value_new = adapt_all(
-        hidden,
-        base_query_proj,
-        base_key_proj,
-        base_value_proj,
-        adapter_down_factors,
-        adapter_up_query,
-        adapter_up_key_value,
-        indicator_matrix,
-        rank_extent,
-    )
-    completed = attend(query, key_cache, value_cache, key_new, value_new, all_lengths)
-    written_keys = write_entry(
-        key_cache[remaining_requests:],
-        key_new[remaining_requests:],
-        all_lengths[remaining_requests:],
-    )
-    written_values = write_entry(
-        value_cache[remaining_requests:],
-        value_new[remaining_requests:],
-        all_lengths[remaining_requests:],
-    )
-    payload = (
-        completed[remaining_requests:],
-        written_keys,
-        written_values,
-        down_rows,
-        upq_rows,
-        upkv_rows,
-    )
-    for bit_level in range(hop_count):
-        moved = shifted(
-            (payload[0], payload[1], payload[2], payload[3], payload[4], payload[5]),
-            "rep",
-            1 << bit_level,
-        )
-        payload = settle(payload, moved, migration_offset, bit_level)
-    (
-        carried_out,
-        moved_keys,
-        moved_values,
-        arrived_down_factors,
-        arrived_up_query,
-        arrived_up_key_value,
-    ) = payload
-    attended = jnp.concatenate([completed[:remaining_requests], carried_out], axis=0)
-    return (
-        attended,
-        moved_keys,
-        moved_values,
-        arrived_down_factors,
-        arrived_up_query,
-        arrived_up_key_value,
-    )
+    positions = key_cache.shape[1]
+    kv_width = base_key_proj.shape[1]
+    replicas = lax.axis_size("rep")
+    me = lax.axis_index("rep")
+    res_row = pick(resident, me)
+
+    offset = [migration_offset[m] for m in range(moving)]
+    place = [
+        sum((offset[k] < offset[m]).astype(jnp.int32) for k in range(moving) if k != m)
+        for m in range(moving)
+    ]
+    slot_at = [sum(jnp.where(place[m] == p, m, 0) for m in range(moving)) for p in range(moving)]
+    offset_at = [
+        sum(jnp.where(place[m] == p, offset[m], 0) for m in range(moving)) for p in range(moving)
+    ]
+
+    def compute():
+        indicator_matrix = (request_adapter_id[:, None] == res_row[None, :]).astype(jnp.float32)
+        own_lengths = lax.dynamic_slice_in_dim(lengths, me * count, count)
+        query, key_new, value_new = adapt_all(
+            hidden,
+            base_query_proj,
+            base_key_proj,
+            base_value_proj,
+            adapter_down_factors,
+            adapter_up_query,
+            adapter_up_key_value,
+            indicator_matrix,
+            rank_extent,
+        )
+        completed = attend(query, key_cache, value_cache, key_new, value_new, own_lengths)
+        return completed, jnp.concatenate([completed, key_new, value_new], axis=1)
+
+    def big_payload(p):
+        row = stay + slot_at[p]
+        mine = pick(request_adapter_id, row)
+        loaded = sum(
+            jnp.where(res_row[n] == mine, n, 0) for n in range(res_row.shape[0])
+        )
+        return (
+            pick(key_cache, row),
+            pick(value_cache, row),
+            pick(adapter_down_factors, loaded),
+            pick(adapter_up_query, loaded),
+            pick(adapter_up_key_value, loaded),
+        )
+
+    def assemble(completed, small, big):
+        rows = []
+        for m in range(moving):
+            row = small[0]
+            for p in range(1, moving):
+                row = jnp.where(place[m] == p, small[p], row)
+            rows.append(row)
+        rows = jnp.stack(rows)
+        width = completed.shape[1]
+        attended = jnp.concatenate([completed[:stay], rows[:, :width]], axis=0)
+
+        def arrange(part):
+            out = []
+            for m in range(moving):
+                chosen = big[0][part]
+                for p in range(1, moving):
+                    chosen = jnp.where(place[m] == p, big[p][part], chosen)
+                out.append(chosen)
+            return jnp.stack(out)
+
+        source = [lax.rem(me - offset[m] + replicas, replicas) for m in range(moving)]
+        spots = jnp.stack([pick(lengths, source[m] * count + stay + m) for m in range(moving)])
+        at = (jnp.arange(positions, dtype=jnp.int32)[None, :] == spots[:, None])[:, :, None]
+        new_keys = rows[:, width : width + kv_width]
+        new_values = rows[:, width + kv_width :]
+        return (
+            attended,
+            jnp.where(at, new_keys[:, None, :], arrange(0)),
+            jnp.where(at, new_values[:, None, :], arrange(1)),
+            arrange(2),
+            arrange(3),
+            arrange(4),
+        )
+
+    table = list(itertools.combinations(range(1, replicas), moving))
+    if len(table) <= MOST_JOINT_BRANCHES:
+
+        def branch(by):
+            def run():
+                big = [
+                    tuple(shifted(part, "rep", by[p]) for part in big_payload(p))
+                    for p in range(moving)
+                ]
+                completed, rows = compute()
+                small = [shifted(pick(rows, stay + slot_at[p]), "rep", by[p]) for p in range(moving)]
+                return assemble(completed, small, big)
+
+            return run
+
+        chosen = sum(
+            jnp.where(
+                jnp.stack([offset_at[p] == by[p] for p in range(moving)]).all(), i, 0
+            )
+            for i, by in enumerate(table)
+        )
+        return lax.switch(chosen, [branch(by) for by in table])
+
+    completed, rows = compute()
+    arrived = []
+    for p in range(moving):
+        payload = (pick(rows, stay + slot_at[p]),) + big_payload(p)
+        for level in range((replicas - 1).bit_length()):
+            payload = lax.cond(
+                jnp.right_shift(offset_at[p], level) % 2 == 1,
+                lambda parts, by=1 << level: tuple(shifted(part, "rep", by) for part in parts),
+                lambda parts: parts,
+                payload,
+            )
+        arrived.append(payload)
+    return assemble(completed, [a[0] for a in arrived], [a[1:] for a in arrived])
 
 
 def solution(mesh):

time: 237 us -> 142 us (0.60)
  the two profiles are of different devices: /device:TPU:0 before, /device:TPU:13 now
where the time goes in v1:
time: 142 us; the launch traced here: 140 us
  waiting for transfers between devices  60.9 us (43%)
  starting transfers between devices  38.1 us (27%)
  local copies, waits for them, and re-layouts  10.6 us (7%)
  other arithmetic  8.27 us (6%)
  matrix products  6.54 us (5%)
  blocking collectives  6.26 us (4%)
  between operations  5.38 us (4%)
  loops' own time  4.12 us (3%)
    ppermute x12, waiting for transfers between devices, shifted(): lax.ppermute(shard, axis, [(i, (i + by) % size) for i in range(size)])  60.9 us
    ppermute x12, starting transfers between devices, shifted(): lax.ppermute(shard, axis, [(i, (i + by) % size) for i in range(size)])  38.1 us
    psum x1, blocking collectives, rank_total(): return lax.psum(partial_rows, 'tp').astype(jnp.bfloat16)  6.26 us
    squeeze x6, local copies, waits for them, and re-layouts, pick(): return lax.dynamic_index_in_dim(array, at, 0, keepdims=False)  5.45 us
    another operation x1, loops' own time, local(): return lax.switch(chosen, [branch(by) for by in table])  4.12 us
    another operation x8, other arithmetic, arrange(): return jnp.stack(out)  3.87 us
    dot_general x3, matrix products, adapter_row_ids(): jnp.einsum('rk,akc->rac', shrunk_part, up_factor, preferred_element_type=...  3.29 us
  transfers between devices with their start and end apart: 12, of which 4 were waited for; matrix products, arithmetic and copies ran while one was open for 13% of the time, Pallas kernels for 0%

profile of v1, /device:TPU:13, one launch (start us, length us, event | category | flops | bytes accessed | tf_op | source)
XLA Modules:
  0.0 140.2 jit_solution(17043280086401158758)
XLA Ops:
  0.6 1.4 fusion.105
  6.8 133.5 %conditional.1 = (bf16[8,2048]{1,0:T(8,128)(2,1)}, bf16[2,512,256]{2,1,0:T(8,128)(2,1)}, bf16[2,512,256]{2,1,0:T(8,128)(2,1)}, bf16[2,2048,192]{1,2,0:T(8,128)(2...) conditional(s32[]{:T(128)} %clamp.3, (s32[]{:T(128)}, s32[32]{0:T(128)}, ...), branch_computations={%region_0.8_spmd, %region_8.0_spmd, %region_16.24_spmd} | conditional | flops 56269736 | bytes 66219776 | solution.py:217
  6.8 0.9 copy.85
  7.8 0.6 slice.116
  8.3 1.3 fusion.99
  12.3 1.5 %dynamic-slice_bitcast_fusion.8 = (bf16[2,64,256]{2,1,0:T(8,128)(2,1)}, bf16[2,64,256]{2,1,0:T(8,128)(2,1)}) fusion(s32[]{:T(128)} %bitcast.24, s32[]{:T(128)} %bitcast.22, bf16[2,2,64,256]{3,2,1,0:T(8,128)(2,1)} %get-tuple-element.316), kind=kLoop, calls=%fused_computation.50 | loop fusion | bytes 262152 | tf_op jit(solution)/shard_map/cond/branch_0_fun/jit(dynamic_index_in_dim)/squeeze | solution.py:93
  13.8 1.3 collective-permute-start.11
  15.1 1.1 collective-permute-start.10
  16.2 0.7 compare_convert_fusion
  16.9 1.9 %fusion.16 = f32[8,192]{1,0:T(8,128)S(1)} fusion(bf16[2,2048,192]{1,2,0:T(8,128)(2,1)} %get-tuple-element.258, bf16[8,2048]{1,0:T(8,128)(2,1)} %get-tuple-element.255, f32[8,2]{0,1:T(2,128)S(1)} %compare_convert_fusion), kind=kOutput, calls=%fused_computation.15 | convolution fusion | flops 12587520 | bytes 1611840 | tf_op jit(solution)/shard_map/cond/branch_0_fun/wb,xbm->wxm/dot_general | solution.py:73
  18.8 6.3 %psum.18 = bf16[8,192]{1,0:T(8,128)(2,1)S(1)} all-reduce(f32[8,192]{1,0:T(8,128)S(1)} %fusion.16), channel_id=1, replica_groups=mesh['pool'=2,'rep'=4,'tp'=4] {'tp'}, use_global_device_ids=true, to_apply=%region_2.2 | all-reduce | flops 1536 | bytes 9216 | tf_op jit(solution)/shard_map/cond/branch_0_fun/psum | solution.py:54
  25.1 1.0 fusion.17
  26.1 0.9 fusion.18
  27.1 0.1 dynamic_slice.112
  27.2 0.1 iota_compare_fusion
  27.3 1.3 fusion.9
  28.7 0.1 fusion.25
  28.8 0.7 select_reduce_fusion
  29.6 0.2 fusion.19
  29.8 0.4 fusion.13
  30.3 0.1 dynamic-slice_reduce_fusion
  30.4 0.4 collective-permute-start.1
  30.8 3.3 %collective-permute-start = (bf16[2560]{0:T(1024)(128)(2,1)S(1)}, bf16[2560]{0:T(1024)(128)(2,1)S(1)}, u32[]{:S(2)}, u32[]{:S(2)}) collective-permute-start(bf16[2560]{0:T(1024)(128)(2,1)S(1)} %get-tuple-element.394), channel_id=1, source_target_pairs={{0,8},{4,12},{8,0},{12,4},{1,9},{5,13},{9,1},{13,5},{2,10},{6,14},... | collective-permute-start | bytes 15368 | tf_op jit(solution)/shard_map/cond/branch_0_fun/ppermute | solution.py:15
  34.1 0.8 dynamic-slice_bitcast_fusion.2
  36.1 1.9 %dynamic-slice_bitcast_fusion.4 = (bf16[512,256]{1,0:T(8,128)(2,1)}, bf16[512,256]{1,0:T(8,128)(2,1)}) fusion(bf16[8,512,256]{2,1,0:T(8,128)(2,1)} %get-tuple-element.273, s32[]{:T(128)S(6)} %select_n.306, s32[]{:T(128)S(6)} %select_n.305), kind=kLoop, calls=%fused_computation.31 | loop fusion | bytes 1048584 | tf_op jit(solution)/shard_map/cond/branch_0_fun/jit(dynamic_index_in_dim)/squeeze | solution.py:93
  38.0 0.2 dynamic-slice_bitcast_fusion
  38.2 0.7 fusion.100
  38.8 1.4 pad_add_fusion
  40.2 0.1 iota_compare_fusion.1
  40.3 1.1 dynamic-slice_bitcast_fusion.6
  41.4 1.4 collective-permute-start.8
  42.8 1.3 collective-permute-start.5
  44.2 0.6 pad_maximum_fusion.4
  44.8 1.0 collective-permute-start.4
  45.9 0.3 collective-permute-start.3
  46.2 0.9 select_bitcast_fusion.9
  47.1 0.7 pad_maximum_fusion.2
  47.7 2.0 %collective-permute-start.2 = (bf16[512,256]{1,0:T(8,128)(2,1)S(1)}, bf16[512,256]{1,0:T(8,128)(2,1)S(1)}, u32[]{:S(2)}, u32[]{:S(2)}) collective-permute-start(bf16[512,256]{1,0:T(8,128)(2,1)S(1)} %get-tuple-element.408), channel_id=1, source_target_pairs={{0,8},{4,12},{8,0},{12,4},{1,9},{5,13},{9,1},{13,5},{2,10},{6,14},... | collective-permute-start | bytes 786440 | tf_op jit(solution)/shard_map/cond/branch_0_fun/ppermute | solution.py:15
  49.7 6.4 %collective-permute-done.8 = bf16[64,2048]{1,0:T(8,128)(2,1)S(1)} collective-permute-done((bf16[64,2048]{1,0:T(8,128)(2,1)}, bf16[64,2048]{1,0:T(8,128)(2,1)S(1)}, u32[]{:S(2)}, u32[]{:S(2)}) %collective-permute-start.8) | collective-permute-done | bytes 262176 | tf_op jit(solution)/shard_map/cond/branch_0_fun/ppermute | solution.py:15
  56.1 22.1 %collective-permute-start.7 = (bf16[2048,192]{0,1:T(8,128)(2,1)S(1)}, bf16[2048,192]{0,1:T(8,128)(2,1)S(1)}, u32[]{:S(2)}, u32[]{:S(2)}) collective-permute-start(bf16[2048,192]{0,1:T(8,128)(2,1)S(1)} %get-tuple-element.411), channel_id=1, source_target_pairs={{0,4},{4,8},{8,12},{12,0},{1,5},{5,9},{9,13},{13,1},{2,6},{6,10},{... | collective-permute-start | bytes 2359304 | tf_op jit(solution)/shard_map/cond/branch_0_fun/ppermute | solution.py:15
  78.3 4.0 %collective-permute-start.6 = (bf16[2048,192]{0,1:T(8,128)(2,1)S(1)}, bf16[2048,192]{0,1:T(8,128)(2,1)S(1)}, u32[]{:S(2)}, u32[]{:S(2)}) collective-permute-start(bf16[2048,192]{0,1:T(8,128)(2,1)S(1)} %get-tuple-element.412), channel_id=1, source_target_pairs={{0,8},{4,12},{8,0},{12,4},{1,9},{5,13},{9,1},{13,5},{2,10},{6,14},... | collective-permute-start | bytes 2359304 | tf_op jit(solution)/shard_map/cond/branch_0_fun/ppermute | solution.py:15
  82.3 0.8 pad_maximum_fusion.1
  83.2 5.1 %collective-permute-done.2 = bf16[512,256]{1,0:T(8,128)(2,1)S(1)} collective-permute-done((bf16[512,256]{1,0:T(8,128)(2,1)S(1)}, bf16[512,256]{1,0:T(8,128)(2,1)S(1)}, u32[]{:S(2)}, u32[]{:S(2)}) %collective-permute-start.2) | collective-permute-done | bytes 262176 | tf_op jit(solution)/shard_map/cond/branch_0_fun/ppermute | solution.py:15
  88.3 1.2 maximum_select_fusion.1
  89.5 32.5 %collective-permute-done.7 = bf16[2048,192]{0,1:T(8,128)(2,1)S(1)} collective-permute-done((bf16[2048,192]{0,1:T(8,128)(2,1)S(1)}, bf16[2048,192]{0,1:T(8,128)(2,1)S(1)}, u32[]{:S(2)}, u32[]{:S(2)}) %collective-permute-start.7) | collective-permute-done | bytes 786464 | tf_op jit(solution)/shard_map/cond/branch_0_fun/ppermute | solution.py:15
  122.0 16.9 %collective-permute-done.6 = bf16[2048,192]{0,1:T(8,128)(2,1)S(1)} collective-permute-done((bf16[2048,192]{0,1:T(8,128)(2,1)S(1)}, bf16[2048,192]{0,1:T(8,128)(2,1)S(1)}, u32[]{:S(2)}, u32[]{:S(2)}) %collective-permute-start.6) | collective-permute-done | bytes 786464 | tf_op jit(solution)/shard_map/cond/branch_0_fun/ppermute | solution.py:15
  138.8 0.1 select_bitcast_fusion.1
  139.0 1.3 pad_maximum_fusion
  (45 shorter events, 0.4 us)
Async XLA Ops:
  6.8 20.3 %copy-start.21 = (s32[32]{0:T(128)S(1)}, s32[32]{0:T(128)}, u32[]{:S(2)}) copy-start(s32[32]{0:T(128)} %get-tuple-element.237) | copy-start | bytes 388 | tf_op jit(solution)/shard_map/cond
  6.8 20.5 %copy-start.18 = (bf16[8,256]{1,0:T(8,128)(2,1)S(1)}, bf16[8,256]{1,0:T(8,128)(2,1)}, u32[]{:S(2)}) copy-start(bf16[8,256]{1,0:T(8,128)(2,1)} %get-tuple-element.276) | copy-start | bytes 12292 | tf_op jit(solution)/shard_map/cond
  6.8 21.8 %copy-start.15 = (bf16[8,256]{1,0:T(8,128)(2,1)S(1)}, bf16[8,256]{1,0:T(8,128)(2,1)}, u32[]{:S(2)}) copy-start(bf16[8,256]{1,0:T(8,128)(2,1)} %get-tuple-element.267) | copy-start | bytes 12292 | tf_op jit(solution)/shard_map/cond
  6.8 21.8 %copy-start.12 = (bf16[8,2048]{1,0:T(8,128)(2,1)S(1)}, bf16[8,2048]{1,0:T(8,128)(2,1)}, u32[]{:S(2)}) copy-start(bf16[8,2048]{1,0:T(8,128)(2,1)} %get-tuple-element.240) | copy-start | bytes 98308 | tf_op jit(solution)/shard_map/cond
  6.8 22.0 %copy-start.3 = (bf16[8,512,256]{2,1,0:T(8,128)(2,1)S(1)}, bf16[8,512,256]{2,1,0:T(8,128)(2,1)}, u32[]{:S(2)}) copy-start(bf16[8,512,256]{2,1,0:T(8,128)(2,1)} %get-tuple-element.264) | copy-start | bytes 6291460 | tf_op jit(solution)/shard_map/cond
  13.8 31.0 %collective-permute-start.11 = (bf16[2,64,256]{2,1,0:T(8,128)(2,1)}, bf16[2,64,256]{2,1,0:T(8,128)(2,1)S(1)}, u32[]{:S(2)}, u32[]{:S(2)}) collective-permute-start(bf16[2,64,256]{2,1,0:T(8,128)(2,1)} %get-tuple-element.423), channel_id=1, source_target_pairs={{0,4},{4,8},{8,12},{12,0},{1,5},{5,9},{9,13},{13,1},{2,6},{6,10},{... | collective-permute-start | bytes 196616 | tf_op jit(solution)/shard_map/cond/branch_0_fun/ppermute | solution.py:15
  15.1 30.8 %collective-permute-start.10 = (bf16[2,64,256]{2,1,0:T(8,128)(2,1)}, bf16[2,64,256]{2,1,0:T(8,128)(2,1)}, u32[]{:S(2)}, u32[]{:S(2)}) collective-permute-start(bf16[2,64,256]{2,1,0:T(8,128)(2,1)} %get-tuple-element.424), channel_id=1, source_target_pairs={{0,8},{4,12},{8,0},{12,4},{1,9},{5,13},{9,1},{13,5},{2,10},{6,14},... | collective-permute-start | bytes 196616 | tf_op jit(solution)/shard_map/cond/branch_0_fun/ppermute | solution.py:15
  27.0 2.8 %copy-start.9 = (bf16[8,512,256]{2,1,0:T(8,128)(2,1)S(1)}, bf16[8,512,256]{2,1,0:T(8,128)(2,1)}, u32[]{:S(2)}) copy-start(bf16[8,512,256]{2,1,0:T(8,128)(2,1)} %get-tuple-element.273) | copy-start | bytes 6291460 | tf_op jit(solution)/shard_map/cond
  29.6 4.5 %copy-start.6 = (bf16[2,64,2048]{2,1,0:T(8,128)(2,1)S(1)}, bf16[2,64,2048]{2,1,0:T(8,128)(2,1)}, u32[]{:S(2)}) copy-start(bf16[2,64,2048]{2,1,0:T(8,128)(2,1)} %get-tuple-element.261) | copy-start | bytes 1572868 | tf_op jit(solution)/shard_map/cond
  29.8 8.1 %copy-start = (bf16[2,2048,192]{1,2,0:T(8,128)(2,1)S(1)}, bf16[2,2048,192]{1,2,0:T(8,128)(2,1)}, u32[]{:S(2)}) copy-start(bf16[2,2048,192]{1,2,0:T(8,128)(2,1)} %get-tuple-element.258) | copy-start | bytes 4718596 | tf_op jit(solution)/shard_map/cond
  30.4 11.0 %collective-permute-start.1 = (bf16[2560]{0:T(1024)(128)(2,1)S(1)}, bf16[2560]{0:T(1024)(128)(2,1)S(1)}, u32[]{:S(2)}, u32[]{:S(2)}) collective-permute-start(bf16[2560]{0:T(1024)(128)(2,1)S(1)} %get-tuple-element.393), channel_id=1, source_target_pairs={{0,4},{4,8},{8,12},{12,0},{1,5},{5,9},{9,13},{13,1},{2,6},{6,10},{... | collective-permute-start | bytes 15368 | tf_op jit(solution)/shard_map/cond/branch_0_fun/ppermute | solution.py:15
  30.8 12.0 %collective-permute-start = (bf16[2560]{0:T(1024)(128)(2,1)S(1)}, bf16[2560]{0:T(1024)(128)(2,1)S(1)}, u32[]{:S(2)}, u32[]{:S(2)}) collective-permute-start(bf16[2560]{0:T(1024)(128)(2,1)S(1)} %get-tuple-element.394), channel_id=1, source_target_pairs={{0,8},{4,12},{8,0},{12,4},{1,9},{5,13},{9,1},{13,5},{2,10},{6,14},... | collective-permute-start | bytes 15368 | tf_op jit(solution)/shard_map/cond/branch_0_fun/ppermute | solution.py:15
  34.9 12.9 %collective-permute-start.9 = (bf16[64,2048]{1,0:T(8,128)(2,1)}, bf16[64,2048]{1,0:T(8,128)(2,1)S(1)}, u32[]{:S(2)}, u32[]{:S(2)}) collective-permute-start(bf16[64,2048]{1,0:T(8,128)(2,1)} %get-tuple-element.415), channel_id=1, source_target_pairs={{0,4},{4,8},{8,12},{12,0},{1,5},{5,9},{9,13},{13,1},{2,6},{6,10},{... | collective-permute-start | bytes 786440 | tf_op jit(solution)/shard_map/cond/branch_0_fun/ppermute | solution.py:15
  41.4 14.7 %collective-permute-start.8 = (bf16[64,2048]{1,0:T(8,128)(2,1)}, bf16[64,2048]{1,0:T(8,128)(2,1)S(1)}, u32[]{:S(2)}, u32[]{:S(2)}) collective-permute-start(bf16[64,2048]{1,0:T(8,128)(2,1)} %get-tuple-element.416), channel_id=1, source_target_pairs={{0,8},{4,12},{8,0},{12,4},{1,9},{5,13},{9,1},{13,5},{2,10},{6,14},... | collective-permute-start | bytes 786440 | tf_op jit(solution)/shard_map/cond/branch_0_fun/ppermute | solution.py:15
  42.8 35.5 %collective-permute-start.5 = (bf16[512,256]{1,0:T(8,128)(2,1)}, bf16[512,256]{1,0:T(8,128)(2,1)S(1)}, u32[]{:S(2)}, u32[]{:S(2)}) collective-permute-start(bf16[512,256]{1,0:T(8,128)(2,1)} %get-tuple-element.405), channel_id=1, source_target_pairs={{0,4},{4,8},{8,12},{12,0},{1,5},{5,9},{9,13},{13,1},{2,6},{6,10},{... | collective-permute-start | bytes 786440 | tf_op jit(solution)/shard_map/cond/branch_0_fun/ppermute | solution.py:15
  44.8 38.3 %collective-permute-start.4 = (bf16[512,256]{1,0:T(8,128)(2,1)}, bf16[512,256]{1,0:T(8,128)(2,1)S(1)}, u32[]{:S(2)}, u32[]{:S(2)}) collective-permute-start(bf16[512,256]{1,0:T(8,128)(2,1)} %get-tuple-element.406), channel_id=1, source_target_pairs={{0,8},{4,12},{8,0},{12,4},{1,9},{5,13},{9,1},{13,5},{2,10},{6,14},... | collective-permute-start | bytes 786440 | tf_op jit(solution)/shard_map/cond/branch_0_fun/ppermute | solution.py:15
  45.9 37.3 %collective-permute-start.3 = (bf16[512,256]{1,0:T(8,128)(2,1)S(1)}, bf16[512,256]{1,0:T(8,128)(2,1)S(1)}, u32[]{:S(2)}, u32[]{:S(2)}) collective-permute-start(bf16[512,256]{1,0:T(8,128)(2,1)S(1)} %get-tuple-element.407), channel_id=1, source_target_pairs={{0,4},{4,8},{8,12},{12,0},{1,5},{5,9},{9,13},{13,1},{2,6},{6,10},{... | collective-permute-start | bytes 786440 | tf_op jit(solution)/shard_map/cond/branch_0_fun/ppermute | solution.py:15
  47.7 40.6 %collective-permute-start.2 = (bf16[512,256]{1,0:T(8,128)(2,1)S(1)}, bf16[512,256]{1,0:T(8,128)(2,1)S(1)}, u32[]{:S(2)}, u32[]{:S(2)}) collective-permute-start(bf16[512,256]{1,0:T(8,128)(2,1)S(1)} %get-tuple-element.408), channel_id=1, source_target_pairs={{0,8},{4,12},{8,0},{12,4},{1,9},{5,13},{9,1},{13,5},{2,10},{6,14},... | collective-permute-start | bytes 786440 | tf_op jit(solution)/shard_map/cond/branch_0_fun/ppermute | solution.py:15
  56.1 65.9 %collective-permute-start.7 = (bf16[2048,192]{0,1:T(8,128)(2,1)S(1)}, bf16[2048,192]{0,1:T(8,128)(2,1)S(1)}, u32[]{:S(2)}, u32[]{:S(2)}) collective-permute-start(bf16[2048,192]{0,1:T(8,128)(2,1)S(1)} %get-tuple-element.411), channel_id=1, source_target_pairs={{0,4},{4,8},{8,12},{12,0},{1,5},{5,9},{9,13},{13,1},{2,6},{6,10},{... | collective-permute-start | bytes 2359304 | tf_op jit(solution)/shard_map/cond/branch_0_fun/ppermute | solution.py:15
  78.3 60.5 %collective-permute-start.6 = (bf16[2048,192]{0,1:T(8,128)(2,1)S(1)}, bf16[2048,192]{0,1:T(8,128)(2,1)S(1)}, u32[]{:S(2)}, u32[]{:S(2)}) collective-permute-start(bf16[2048,192]{0,1:T(8,128)(2,1)S(1)} %get-tuple-element.412), channel_id=1, source_target_pairs={{0,8},{4,12},{8,0},{12,4},{1,9},{5,13},{9,1},{13,5},{2,10},{6,14},... | collective-permute-start | bytes 2359304 | tf_op jit(solution)/shard_map/cond/branch_0_fun/ppermute | solution.py:15
